TPU v7x, 256 devices: a whole 4x4x8 slice. The times are simulated.
256 devices in a mesh: store: 64 (over x, y_hi, z), grid: 2 (over core), row: 2 (over y_lo).
Axes of the slice: x: 4, y: 4 (y_hi: 2, y_lo: 2; y = y_hi * 2 + y_lo), z: 8, core: 2. Of those that a mesh axis runs over, the one named last changes fastest.
Arguments:
- embeddings: bfloat16 [131072, 768], P('store'), may hold values from -6 to 6
- members: int32 [4, 16384], replicated, may hold values from 0 to 131071, as said below
- order: int32 [4, 16384], replicated, may hold values from 0 to 16383, each once within a row
- sizes: int32 [4], replicated, may hold values from 8192 to 16384, as said below
Outputs:
- best: float32 [65536], P(('store', 'grid', 'row'))
Inputs may be any that keep to these rules, and one draw needn't show every extreme that they name: `members`: all ids are distinct. Each cluster's slots fall into aligned blocks of 256 slots, and within each block exactly 4 ids lie in each storage shard of 2048 rows. `sizes`: one cluster fills all 16384 slots.
All inputs are finite; a program needn't handle non-finite values.
Results may differ from a plain program's by a relative error of at most 0.0012.
Values may be sent and summed in bfloat16 or wider, within the bound.
A program may use at most 128 MiB of HBM per device.

v0:
```python
import jax
import jax.numpy as jnp
from jax import lax
from jax.sharding import PartitionSpec as P

MEM_DEV = 256
CLUS = 4


def from_partner(block, axis, bit):
    count = lax.axis_size(axis)
    route = []
    for low in range(count):
        high = low | 1 << bit
        if high != low and high < count:
            route += [(low, high), (high, low)]
    return lax.ppermute(block, axis, route)


def join_pair(stack, partner, upper):
    return jnp.where(
        upper == 0,
        jnp.concatenate([stack, partner], axis=0),
        jnp.concatenate([partner, stack], axis=0),
    )


def on_device(embeddings, members, order, sizes):
    n_store = lax.axis_size("store")
    group = n_store // CLUS
    bits = group.bit_length() - 1
    store_pos = lax.axis_index("store")
    grid_pos = lax.axis_index("grid")
    row_pos = lax.axis_index("row")
    cluster = store_pos // group
    local_store = store_pos % group
    share = MEM_DEV // n_store
    rows_dev = embeddings.shape[0]
    width = embeddings.shape[1]
    plane = grid_pos * 2 + row_pos
    blocks = members.reshape(n_store, 4, MEM_DEV)
    wanted = lax.dynamic_index_in_dim(blocks, plane, 1, keepdims=False)
    local_ids = wanted - store_pos * rows_dev
    mine = (local_ids >= 0) & (local_ids < rows_dev)
    rank = jnp.cumsum(mine.astype(jnp.int32), axis=1) - 1
    places = jnp.arange(share, dtype=jnp.int32)
    picked = mine[:, None, :] & (rank[:, None, :] == places[None, :, None])
    select = jnp.sum(jnp.where(picked, local_ids[:, None, :], 0), axis=2)
    outgoing = embeddings[select]
    incoming = lax.all_to_all(outgoing, "store", split_axis=0, concat_axis=0, tiled=True)
    my_ids = lax.dynamic_index_in_dim(wanted, store_pos, 0, keepdims=False)
    source = my_ids // rows_dev
    onehot = (source[:, None] == jnp.arange(n_store, dtype=jnp.int32)[None, :]).astype(jnp.int32)
    before = jnp.cumsum(onehot, axis=0) - 1
    rank_in = jnp.sum(onehot * before, axis=1)
    arrived = incoming.reshape(n_store * share, width)[source * share + rank_in]
    vector = arrived.astype(jnp.float32)
    scale = lax.rsqrt(jnp.sum(vector * vector, axis=1, keepdims=True) + 1e-06)
    unit = (vector * scale).astype(jnp.bfloat16)
    cap = members.shape[1]
    flat_order = lax.dynamic_index_in_dim(order, cluster, 0, keepdims=False)
    cluster_order = flat_order.reshape(group, 2, 2, MEM_DEV)
    slot_table = jnp.arange(cap, dtype=jnp.int32).reshape(group, 2, 2, MEM_DEV)
    count = lax.dynamic_index_in_dim(sizes, cluster, 0, keepdims=False)
    own_slots = lax.dynamic_index_in_dim(
        lax.dynamic_index_in_dim(slot_table[local_store], grid_pos, 0, keepdims=False),
        row_pos,
        0,
        keepdims=False,
    )

    def pick_rows(table):
        return jnp.transpose(table, (1, 0, 2, 3)).reshape(-1)

    own_order = lax.dynamic_index_in_dim(
        lax.dynamic_index_in_dim(cluster_order[local_store], grid_pos, 0, keepdims=False),
        row_pos,
        0,
        keepdims=False,
    )
    stack = lax.all_gather(unit[None], "row", axis=0, tiled=True)[None]
    for bit in range(bits):
        partner = from_partner(stack, "store", bit)
        stack = join_pair(stack, partner, local_store >> bit & 1)
    start_best = jnp.full((unit.shape[0],), -1.0, jnp.float32)
    keys = lax.all_gather(stack[None], "grid", axis=0, tiled=True).reshape(-1, width)
    key_order = pick_rows(cluster_order)
    key_slots = pick_rows(slot_table)
    score = lax.dot_general(
        unit, keys, (((1,), (1,)), ((), ())), preferred_element_type=jnp.float32
    )
    mask = (key_slots < count)[None, :] & (key_order[None, :] < own_order[:, None])
    own_best = jnp.maximum(start_best, jnp.max(jnp.where(mask, score, -1.0), axis=1))
    return jnp.where(own_slots < count, own_best, 0.0)


def solution(mesh):
    return jax.shard_map(
        on_device,
        mesh=mesh,
        in_specs=(P("store", None), P(), P(), P()),
        out_specs=P(("store", "grid", "row")),
        check_vma=False,
    )
```

profile of v0, /device:TPU:1, one launch (start us, length us, event | category | flops | bytes accessed | tf_op | source)
XLA Modules:
  0.0 508.2 jit_solution(16044870054045756605)
XLA Ops:
  6.5 1.3 reshape.433
  7.9 0.8 fusion.13
  8.7 0.6 reduce-window.14
  9.3 0.2 slice_reduce_fusion.1
  9.5 0.1 copy_bitcast_fusion
  9.6 0.9 copy.31
  10.5 0.2 select_reduce_fusion
  10.7 0.1 copy.19
  10.8 0.1 reshape.444
  10.9 1.2 gather_fusion
  12.1 0.8 reshape.443
  12.9 15.1 %all-to-all-start = ((bf16[64,4,768]{2,1,0:T(4,128)(2,1)}), bf16[64,4,768]{2,1,0:T(4,128)(2,1)S(1)}, u32[]{:S(2)}, u32[]{:S(2)}) async-start(bf16[64,4,768]{2,1,0:T(4,128)(2,1)} %reshape.443), calls=%async_computation | async-start | bytes 786432 | tf_op jit(solution)/shard_map/all_to_all | solution.py:50
  28.0 0.0 all-gather.2.cloned.1.call-start
  28.1 0.7 constant_dynamic-slice_fusion
  28.8 0.6 reduce-window.16
  29.4 0.2 slice_reduce_fusion
  29.7 0.1 fusion.9
  29.8 0.7 compare_select_fusion
  30.5 13.0 %all-to-all-done = bf16[64,4,768]{2,1,0:T(4,128)(2,1)S(1)} async-done(((bf16[64,4,768]{2,1,0:T(4,128)(2,1)}), bf16[64,4,768]{2,1,0:T(4,128)(2,1)S(1)}, u32[]{:S(2)}, u32[]{:S(2)}) %all-to-all-start) | async-done | bytes 393248 | tf_op jit(solution)/shard_map/all_to_all | solution.py:50
  43.4 0.1 reshape.435
  43.5 1.2 gather_fusion.1
  44.7 0.2 fusion.1
  44.9 0.6 copy-done.4
  45.5 0.1 fusion.4
  45.6 8.3 %all_gather.6 = bf16[2,256,768]{2,1,0:T(8,128)(2,1)S(1)} all-gather(bf16[1,256,768]{2,1,0:T(8,128)(2,1)S(1)} %fusion.4), channel_id=1, replica_groups=mesh['store'=64,'grid'=2,'row'=2] {'row'}, dimensions={0}, use_global_device_ids=true | all-gather | bytes 1179648 | tf_op jit(solution)/shard_map/all_gather | solution.py:81
  53.9 2.2 collective-permute-start
  56.1 14.4 %collective-permute-done = bf16[1,2,256,768]{3,2,1,0:T(8,128)(2,1)S(1)} collective-permute-done((bf16[1,2,256,768]{3,2,1,0:T(8,128)(2,1)S(1)}, bf16[1,2,256,768]{3,2,1,0:T(8,128)(2,1)S(1)}, u32[]{:S(2)}, u32[]{:S(2)}) %collective-permute-start) | collective-permute-done | bytes 786464 | tf_op jit(solution)/shard_map/ppermute | solution.py:17
  70.5 0.3 maximum_select_fusion.3
  70.7 3.3 collective-permute-start.1
  74.0 67.1 %collective-permute-done.1 = bf16[2,2,256,768]{3,2,1,0:T(8,128)(2,1)} collective-permute-done((bf16[2,2,256,768]{3,2,1,0:T(8,128)(2,1)S(1)}, bf16[2,2,256,768]{3,2,1,0:T(8,128)(2,1)}, u32[]{:S(2)}, u32[]{:S(2)}) %collective-permute-start.1) | collective-permute-done | bytes 1572896 | tf_op jit(solution)/shard_map/ppermute | solution.py:17
  141.2 3.1 maximum_select_fusion.2
  144.3 3.1 collective-permute-start.2
  147.4 138.2 %collective-permute-done.2 = bf16[4,2,256,768]{3,2,1,0:T(8,128)(2,1)} collective-permute-done((bf16[4,2,256,768]{3,2,1,0:T(8,128)(2,1)S(1)}, bf16[4,2,256,768]{3,2,1,0:T(8,128)(2,1)}, u32[]{:S(2)}, u32[]{:S(2)}) %collective-permute-start.2) | collective-permute-done | bytes 3145760 | tf_op jit(solution)/shard_map/ppermute | solution.py:17
  285.7 7.0 %maximum_select_fusion.1 = bf16[8,2,256,768]{3,2,1,0:T(8,128)(2,1)} fusion(bf16[4,2,256,768]{3,2,1,0:T(8,128)(2,1)} %collective-permute-done.2, bf16[4,2,256,768]{3,2,1,0:T(8,128)(2,1)S(1)} %maximum_select_fusion.2, pred[]{:T(512)S(6)} %eq.58), kind=kLoop, calls=%fused_computation.4 | loop fusion | flops 9437184 | bytes 12582913 | tf_op jit(solution)/shard_map/jit(_where)/select_n | solution.py:21
  292.6 138.4 %collective-permute-done.3 = bf16[8,2,256,768]{3,2,1,0:T(8,128)(2,1)} collective-permute-done((bf16[8,2,256,768]{3,2,1,0:T(8,128)(2,1)}, bf16[8,2,256,768]{3,2,1,0:T(8,128)(2,1)}, u32[]{:S(2)}, u32[]{:S(2)}) %collective-permute-start.3) | collective-permute-done | bytes 6291488 | tf_op jit(solution)/shard_map/ppermute | solution.py:17
  431.1 13.8 %maximum_select_fusion = bf16[1,16,2,256,768]{4,3,2,1,0:T(8,128)(2,1)} fusion(bf16[1,8,2,256,768]{4,3,2,1,0:T(8,128)(2,1)} %bitcast.14, bf16[1,8,2,256,768]{4,3,2,1,0:T(8,128)(2,1)} %bitcast.13, pred[]{:T(512)S(6)} %eq.57), kind=kLoop, calls=%fused_computation.3 | loop fusion | flops 18874368 | bytes 25165824 | tf_op jit(solution)/shard_map/jit(_where)/select_n | solution.py:21
  444.9 0.0 all-gather.2.cloned.1.call-update
  444.9 0.6 copy-done.5
  445.5 0.6 dynamic_slice.29
  446.1 1.1 dynamic-slice_reduce_fusion
  447.3 0.7 copy.25
  448.0 0.7 add_compare_fusion
  448.7 0.1 reshape.439
  448.7 1.2 compare_reduce_fusion
  450.0 0.6 constant_dynamic-slice_fusion.1
  450.5 36.6 %all-gather.2.cloned.1.call-done = bf16[2,16,2,256,768]{4,3,2,1,0:T(8,128)(2,1)} async-done(((bf16[1,16,2,256,768]{4,3,2,1,0:T(8,128)(2,1)}), bf16[2,16,2,256,768]{4,3,2,1,0:T(8,128)(2,1)}) %all-gather.2.cloned.1.call-update) | async-done | bytes 25165840 | tf_op jit(solution)/shard_map/all_gather | solution.py:86
  487.1 13.0 %fusion = f32[256]{0:T(256)} fusion(bf16[16384,768]{1,0:T(8,128)(2,1)} %bitcast.74, s32[256]{0:T(256)} %bitcast.73, s32[16384]{0:T(1024)} %bitcast.68, pred[16384]{0:T(1024)(128)(4,1)S(1)} %reshape.439, bf16[256,768]{1,0:T(8,128)(2,1)S(1)} %gather_fusion.1, f32[256]{0:T(256)} %copy-done.4), kind=kOutput, calls=%fused_computation.5 | convolution fusion | flops 6459817984 | bytes 25644032 | tf_op jit(solution)/shard_map/dot_general | solution.py:89
  500.1 1.2 maximum_select_fusion.4
  (26 shorter events, 0.2 us)
Async XLA Ops:
  6.5 4.3 copy-start
  7.9 0.8 copy-start.3
  12.9 30.5 %all-to-all-start = ((bf16[64,4,768]{2,1,0:T(4,128)(2,1)}), bf16[64,4,768]{2,1,0:T(4,128)(2,1)S(1)}, u32[]{:S(2)}, u32[]{:S(2)}) async-start(bf16[64,4,768]{2,1,0:T(4,128)(2,1)} %reshape.443), calls=%async_computation | async-start | bytes 786432 | tf_op jit(solution)/shard_map/all_to_all | solution.py:50
  28.0 459.1 %all-gather.2.cloned.1.call-start = ((), (), s32[]{:S(2)}) async-start(), calls=%async_computation.1 | async-start | bytes 37748736 | tf_op jit(solution)/shard_map/all_gather | solution.py:86
  44.9 0.6 copy-start.4
  53.9 16.6 %collective-permute-start = (bf16[1,2,256,768]{3,2,1,0:T(8,128)(2,1)S(1)}, bf16[1,2,256,768]{3,2,1,0:T(8,128)(2,1)S(1)}, u32[]{:S(2)}, u32[]{:S(2)}) collective-permute-start(bf16[1,2,256,768]{3,2,1,0:T(8,128)(2,1)S(1)} %bitcast.61), channel_id=1, source_target_pairs={{0,4},{4,0},{8,12},{12,8},{16,20},{20,16},{24,28},{28,24},{32,36},... | collective-permute-start | bytes 2359304 | tf_op jit(solution)/shard_map/ppermute | solution.py:17
  70.7 3.3 copy-start.2
  70.7 70.5 %collective-permute-start.1 = (bf16[2,2,256,768]{3,2,1,0:T(8,128)(2,1)S(1)}, bf16[2,2,256,768]{3,2,1,0:T(8,128)(2,1)}, u32[]{:S(2)}, u32[]{:S(2)}) collective-permute-start(bf16[2,2,256,768]{3,2,1,0:T(8,128)(2,1)S(1)} %maximum_select_fusion.3), channel_id=1, source_target_pairs={{0,8},{8,0},{4,12},{12,4},{16,24},{24,16},{20,28},{28,20},{32,40},... | collective-permute-start | bytes 4718600 | tf_op jit(solution)/shard_map/ppermute | solution.py:17
  144.3 141.4 %collective-permute-start.2 = (bf16[4,2,256,768]{3,2,1,0:T(8,128)(2,1)S(1)}, bf16[4,2,256,768]{3,2,1,0:T(8,128)(2,1)}, u32[]{:S(2)}, u32[]{:S(2)}) collective-permute-start(bf16[4,2,256,768]{3,2,1,0:T(8,128)(2,1)S(1)} %maximum_select_fusion.2), channel_id=1, source_target_pairs={{0,16},{16,0},{4,20},{20,4},{8,24},{24,8},{12,28},{28,12},{32,48},... | collective-permute-start | bytes 9437192 | tf_op jit(solution)/shard_map/ppermute | solution.py:17
  292.6 138.4 %collective-permute-start.3 = (bf16[8,2,256,768]{3,2,1,0:T(8,128)(2,1)}, bf16[8,2,256,768]{3,2,1,0:T(8,128)(2,1)}, u32[]{:S(2)}, u32[]{:S(2)}) collective-permute-start(bf16[8,2,256,768]{3,2,1,0:T(8,128)(2,1)} %maximum_select_fusion.1), channel_id=1, source_target_pairs={{0,32},{32,0},{4,36},{36,4},{8,40},{40,8},{12,44},{44,12},{16,48},... | collective-permute-start | bytes 18874376 | tf_op jit(solution)/shard_map/ppermute | solution.py:17
  444.9 0.7 copy-start.5
  487.1 14.2 %copy-start.1 = (bf16[2048,768]{1,0:T(8,128)(2,1)S(1)}, bf16[2048,768]{1,0:T(8,128)(2,1)}, u32[]{:S(2)}) copy-start(bf16[2048,768]{1,0:T(8,128)(2,1)} %param.4) | copy-start | bytes 9437188
Sparse Core Ops, SparseCore 0:
  445.0 42.0 all-gather.1
where the time goes:
time: 509 us; the launch traced here: 508 us
  waiting for transfers between devices  408 us (80%)
  other arithmetic  30.8 us (6%)
  starting transfers between devices  23.8 us (5%)
  between operations  13.6 us (3%)
  matrix products  13 us (3%)
  local copies, waits for them, and re-layouts  11 us (2%)
  blocking collectives  8.27 us (2%)
    ppermute x4, waiting for transfers between devices, from_partner(): return lax.ppermute(block, axis, route)  358 us
    all_gather x1, waiting for transfers between devices, on_device(): lax.all_gather(stack[None], 'grid', axis=0, tiled=True).reshape(-1, width)  36.6 us
    select_n x4, other arithmetic, join_pair(): jnp.where(upper == 0, jnp.concatenate([stack, partner], axis=0), jnp.conc...  24.2 us
    all_to_all x1, starting transfers between devices, on_device(): lax.all_to_all(outgoing, 'store', split_axis=0, concat_axis=0, tiled=True)  15.1 us
    dot_general x1, matrix products, on_device(): lax.dot_general(unit, keys, (((1,), (1,)), ((), ())), preferred_element_t...  13 us
    all_to_all x1, waiting for transfers between devices, on_device(): lax.all_to_all(outgoing, 'store', split_axis=0, concat_axis=0, tiled=True)  13 us
  transfers between devices with their start and end apart: 6, of which 6 were waited for; matrix products, arithmetic and copies ran while one was open for 1% of the time, Pallas kernels for 0%

commit v1 on v0

v1 whole, which is shorter than its diff:
```python
import jax
import jax.numpy as jnp
from jax import lax
from jax.experimental import pallas as pl
from jax.experimental.pallas import tpu as pltpu
from jax.sharding import PartitionSpec as P

NZ_SLOTS = 10
OWN, X, W, V = 4, 10, 11, 12
N_SLOTS = 13
D = 768
MEM = 256
PIECE = 64
NEVER = float(1 << 20)
MESH = pl.DeviceIdType.MESH
F32 = jnp.float32
SLOT_AT = [((0, z), c) for z in range(-2, 3) for c in (0, 1)] + [((1, -1), 0), ((-1, -2), 0), ((2, -2), 0)]
ROW_SLOTS = (4, 6, 0, X, W, V)


def coordinates():
    store = lax.axis_index("store")
    return store // 16, (store // 8) % 2, store % 8, lax.axis_index("grid"), lax.axis_index("row")


def device(x, y_hi, z, core, y_lo):
    return (x * 16 + y_hi * 8 + z, core, y_lo)


def spread(row):
    return jnp.transpose(jnp.broadcast_to(row, (128, 128)))


def kernel(emb_hbm, members_hbm, order_hbm, sizes, out, emb, members, order, table, held, give, vec, col_ord, row_ord, col_best, row_best, part, mine, got, load_sem, send_sem, recv_sem, part_send, part_recv, route_send, route_recv):
    x, y_hi, z, core, y_lo = coordinates()
    y = y_hi * 2 + y_lo
    store = x * 16 + y_hi * 8 + z

    def at(dx, dz, other=0):
        side = core if other == 0 else 1 - core
        return device((x + dx + 4) % 4, y_hi, (z + dz + 8) % 8, side, y_lo)

    partner = device(x, 1 - y_hi, z, core, 1 - y_lo)
    greet = [at(0, 1), at(0, -1), at(1, 0), at(-1, 0), at(2, 0), at(0, 0, 1)]
    greet += [partner, device(x, y_hi, z, core, 1 - y_lo), device(x, 1 - y_hi, z, core, y_lo)]
    barrier = pltpu.get_barrier_semaphore()
    for one in greet:
        pl.semaphore_signal(barrier, inc=1, device_id=one, device_id_type=MESH)

    loads = [
        pltpu.make_async_copy(members_hbm, members, load_sem.at[0]),
        pltpu.make_async_copy(order_hbm, order, load_sem.at[1]),
        pltpu.make_async_copy(emb_hbm, emb, load_sem.at[2]),
    ]
    for one in loads:
        one.start()
    loads[0].wait()
    loads[1].wait()

    def lay(ref, cluster, where):
        for b in range(PIECE):
            line = ref[pl.ds(cluster, 1), b * MEM : (b + 1) * MEM]
            table[where, b : b + 1, :] = line
            table[where, PIECE + b : PIECE + b + 1, :] = line

    lay(members, y, 0)
    lay(members, 3 - y, 1)
    lay(order, y, 2)
    ids = jnp.transpose(table[0])
    ids_partner = jnp.transpose(table[1])
    slot = lax.broadcasted_iota(jnp.int32, (MEM, 128), 0) + MEM * (lax.broadcasted_iota(jnp.int32, (MEM, 128), 1) % PIECE)
    rank_of = jnp.where(slot < sizes[y], jnp.transpose(table[2]).astype(F32), NEVER)
    upper = lax.broadcasted_iota(jnp.int32, (1, 128), 1) // PIECE
    before = (
        lax.broadcasted_iota(jnp.int32, (MEM, MEM), 1) < lax.broadcasted_iota(jnp.int32, (MEM, MEM), 0)
    ).astype(jnp.bfloat16)

    def ranks(local):
        inside = (local >= 0) & (local < 2048)
        count = jnp.dot(before, jnp.where(inside, 1.0, 0.0).astype(jnp.bfloat16), preferred_element_type=F32)
        return jnp.where(inside, count, -1.0)

    def pick(rank, side, values):
        wanted = (2 * side + upper).astype(F32)
        return jnp.sum(jnp.where(rank == wanted, values, 0.0), axis=0, keepdims=True)

    chosen = []
    for table_ids in (ids, ids_partner):
        local = table_ids - store * 2048
        chosen.append(spread(pick(ranks(local), core, local.astype(F32))).astype(jnp.int32))
    loads[2].wait()
    lane = lax.broadcasted_iota(jnp.int32, (128, 128), 1)
    for half in range(2):
        onehot = jnp.concatenate([jnp.where(chosen[half] == lane + 128 * j, 1.0, 0.0).astype(jnp.bfloat16) for j in range(16)], axis=1)
        for n in range(3):
            vec[:, n * 256 : (n + 1) * 256] = jnp.dot(onehot, emb[:, n * 256 : (n + 1) * 256], preferred_element_type=F32)
        vector = vec[...]
        scale = lax.rsqrt(jnp.sum(vector * vector, axis=1, keepdims=True) + 1e-06)
        unit = (vector * scale).astype(jnp.bfloat16).reshape(2, PIECE, D)
        if half == 0:
            held[pl.ds(OWN * 4 + y_hi * 2, 2)] = unit
        else:
            give[...] = unit

    pl.semaphore_wait(barrier, len(greet))

    def piece(slot, q):
        half, rr = q // 2, q % 2
        side = y_hi if half == 0 else 1 - y_hi
        return slot * 4 + side * 2 + rr

    def send(src_slot, dst_slot, q, to):
        pltpu.make_async_remote_copy(
            held.at[piece(src_slot, q)],
            held.at[piece(dst_slot, q)],
            send_sem.at[0],
            recv_sem.at[dst_slot * 4 + q],
            device_id=to,
            device_id_type=MESH,
        ).start()

    def arrived(slot, q):
        one = held.at[piece(slot, q)]
        pltpu.make_async_remote_copy(
            one, one, send_sem.at[0], recv_sem.at[slot * 4 + q], device_id=at(0, 1), device_id_type=MESH
        ).wait_recv()

    def send_own(q):
        send(OWN, 2, q, at(0, 1))
        send(OWN, 6, q, at(0, -1))
        send(OWN, 5, q, at(0, 0, 1))

    def step_near(q):
        arrived(2, q)
        send(2, 0, q, at(0, 1))
        send(2, X, q, at(-1, 0))
        send(2, 3, q, at(0, 0, 1))
        arrived(6, q)
        send(6, 8, q, at(0, -1))
        send(6, 7, q, at(0, 0, 1))

    def step_far(q):
        arrived(0, q)
        send(0, W, q, at(1, 0))
        send(0, V, q, at(2, 0))
        send(0, 1, q, at(0, 0, 1))
        arrived(8, q)
        send(8, 9, q, at(0, 0, 1))

    for rr in range(2):
        pltpu.make_async_remote_copy(
            give.at[rr],
            held.at[OWN * 4 + y_hi * 2 + rr],
            send_sem.at[0],
            recv_sem.at[OWN * 4 + 2 + rr],
            device_id=partner,
            device_id_type=MESH,
        ).start()
    send_own(0)
    send_own(1)

    def block_order(dx, dz):
        rows = []
        for hi in range(2):
            shard = ((x + dx + 4) % 4) * 16 + hi * 8 + (z + dz + 8) % 8
            rows.append(ranks(ids - shard * 2048))
        return rows

    for s in range(N_SLOTS):
        (dx, dz), other = SLOT_AT[s]
        if other == 0:
            both = block_order(dx, dz)
        side = core if other == 0 else 1 - core
        for hi in range(2):
            line = pick(both[hi], side, rank_of)
            if s < NZ_SLOTS:
                col_ord[s, :, hi * 128 : (hi + 1) * 128] = jnp.broadcast_to(line, (8, 128))
            if s in ROW_SLOTS:
                row_ord[ROW_SLOTS.index(s), hi * 128 : (hi + 1) * 128, :] = spread(line)
    col_best[...] = jnp.full(col_best.shape, -1.0, F32)
    row_best[...] = jnp.full(row_best.shape, -1.0, F32)

    def product(left, right, full):
        where = ROW_SLOTS.index(left)
        a = held[left * 4 : left * 4 + 4].reshape(MEM, D)
        b = held[pl.ds(right * 4, 4)].reshape(MEM, D)
        score = lax.dot_general(a, b, (((1,), (1,)), ((), ())), preferred_element_type=F32)
        own = row_ord[where]
        own = jnp.concatenate([own, own], axis=1)
        other = col_ord[right][0:1, :]
        earlier = other < own
        for_rows = jnp.where(earlier, score, -1.0)
        row_best[where] = jnp.maximum(row_best[where], jnp.maximum(for_rows[:, :128], for_rows[:, 128:]))
        if full:
            for_cols = jnp.where(earlier, -1.0, score)
            col_best[right] = jnp.maximum(col_best[right], jnp.max(for_cols.reshape(32, 8, MEM), axis=0))

    def products(left, first, last, full):
        def one(right, carry):
            product(left, right, full)
            return carry

        lax.fori_loop(first, last, one, 0)

    step_near(0)
    step_near(1)
    arrived(OWN, 2)
    send_own(2)
    step_far(0)
    arrived(OWN, 3)
    send_own(3)
    step_far(1)
    step_near(2)
    step_near(3)
    for q in range(4):
        arrived(5, q)
    products(OWN, 4, 6, False)
    step_far(2)
    step_far(3)
    for q in range(4):
        arrived(7, q)
        arrived(9, q)
    products(OWN, 6, 10, True)
    for q in range(4):
        arrived(1, q)
    products(6, 0, 2, True)
    products(0, 8, 10, False)
    for q in range(4):
        arrived(X, q)
        arrived(3, q)
    products(X, 0, 10, True)
    for q in range(4):
        arrived(W, q)
    products(W, 4, 10, True)
    for q in range(4):
        arrived(V, q)
    products(V, 2, 8, True)
    products(V, 0, 2, False)
    products(V, 8, 10, False)

    sends = []
    for s in range(N_SLOTS):
        (dx, dz), other = SLOT_AT[s]
        for hi in range(2):
            line = jnp.full((1, 128), -1.0, F32)
            if s in ROW_SLOTS:
                line = jnp.max(jnp.transpose(row_best[ROW_SLOTS.index(s), hi * 128 : (hi + 1) * 128, :]), axis=0, keepdims=True)
            if s < NZ_SLOTS:
                line = jnp.maximum(line, jnp.max(col_best[s, :, hi * 128 : (hi + 1) * 128], axis=0, keepdims=True))
            if s == OWN:
                mine[hi : hi + 1, :] = line
            else:
                part[0, s, hi : hi + 1, :] = line
        if s != OWN:
            pltpu.make_async_remote_copy(
                part.at[0, s],
                part.at[1, s],
                part_send.at[0],
                part_recv.at[0],
                device_id=at(dx, dz, other),
                device_id_type=MESH,
            ).start()
    twelve = part.at[0, pl.ds(0, N_SLOTS - 1)]
    back = pltpu.make_async_remote_copy(twelve, twelve, part_send.at[0], part_recv.at[0], device_id=at(0, 1), device_id_type=MESH)
    back.wait_recv()
    best = mine[...]
    for s in range(N_SLOTS):
        if s != OWN:
            best = jnp.maximum(best, part[1, s])
    mine[...] = best
    back.wait_send()

    sender = (x * 8 + z) * 2 + core

    def route(b, carry):
        to_hi, to_z, to_core, to_lo = b // 32, (b // 4) % 8, (b // 2) % 2, b % 2
        self_there = (x == y) & (to_hi == y_hi) & (to_z == z) & (to_core == core) & (to_lo == y_lo)

        @pl.when(self_there)
        def _():
            pltpu.make_async_copy(mine, got.at[sender], route_recv.at[0]).start()

        @pl.when(jnp.logical_not(self_there))
        def _():
            pltpu.make_async_remote_copy(
                mine,
                got.at[sender],
                route_send.at[0],
                route_recv.at[0],
                device_id=device(y, to_hi, to_z, to_core, to_lo),
                device_id_type=MESH,
            ).start()

        return carry

    lax.fori_loop(0, 64, route, 0)

    block = ((y_hi * 8 + z) * 2 + core) * 2 + y_lo
    own_ids = members[pl.ds(x, 1), pl.ds(pl.multiple_of(block * MEM, MEM), MEM)]
    shard = own_ids // 2048
    shard_rows = jnp.concatenate([spread(shard[:, :128].astype(F32)), spread(shard[:, 128:].astype(F32))], axis=0)
    shard_rows = jnp.concatenate([shard_rows, shard_rows], axis=1)
    same = (shard_rows == shard.astype(F32)) & (
        lax.broadcasted_iota(jnp.int32, (MEM, MEM), 0) < lax.broadcasted_iota(jnp.int32, (MEM, MEM), 1)
    )
    rank = jnp.sum(jnp.where(same, 1.0, 0.0), axis=0, keepdims=True).astype(jnp.int32)
    from_sender = ((shard // 16) * 8 + shard % 8) * 2 + rank // 2
    from_place = ((shard // 8) % 2) * 2 + rank % 2
    from_which = from_sender * 4 + from_place

    total = got
    land = pltpu.make_async_remote_copy(total, total, route_send.at[0], route_recv.at[0], device_id=at(0, 1), device_id_type=MESH)
    land.wait_recv()
    value = jnp.zeros((1, MEM), F32)
    senders = lax.broadcasted_iota(jnp.int32, (64, MEM), 0)
    lanes = lax.broadcasted_iota(jnp.int32, (64, 128), 1)
    for hi in range(2):
        rows = got[:, hi, :]
        for rr in range(2):
            column = jnp.sum(jnp.where(lanes == rr * PIECE + block, rows, 0.0), axis=1, keepdims=True)
            here = from_which == senders * 4 + (hi * 2 + rr)
            value = value + jnp.sum(jnp.where(here, column, 0.0), axis=0, keepdims=True)
    slots = block * MEM + lax.broadcasted_iota(jnp.int32, (1, MEM), 1)
    out[...] = jnp.where(slots < sizes[x], value, 0.0)

    sent = held.at[pl.ds(0, 50)]
    pltpu.make_async_remote_copy(sent, sent, send_sem.at[0], recv_sem.at[0], device_id=at(0, 1), device_id_type=MESH).wait_send()

    @pl.when(x == y)
    def _():
        fewer = got.at[pl.ds(0, 63)]
        pltpu.make_async_remote_copy(fewer, fewer, route_send.at[0], route_recv.at[0], device_id=at(0, 1), device_id_type=MESH).wait_send()

    @pl.when(x != y)
    def _():
        pltpu.make_async_remote_copy(total, total, route_send.at[0], route_recv.at[0], device_id=at(0, 1), device_id_type=MESH).wait_send()


def on_device(embeddings, members, order, sizes):
    vmem = pltpu.VMEM
    dma = pltpu.SemaphoreType.DMA
    best = pl.pallas_call(
        kernel,
        out_shape=jax.ShapeDtypeStruct((1, MEM), F32),
        in_specs=[pl.BlockSpec(memory_space=pl.ANY)] * 3 + [pl.BlockSpec(memory_space=pltpu.SMEM)],
        out_specs=pl.BlockSpec(memory_space=pltpu.VMEM),
        scratch_shapes=[
            vmem((2048, D), jnp.bfloat16),
            vmem((4, 16384), jnp.int32),
            vmem((4, 16384), jnp.int32),
            vmem((3, 128, MEM), jnp.int32),
            vmem((N_SLOTS * 4, PIECE, D), jnp.bfloat16),
            vmem((2, PIECE, D), jnp.bfloat16),
            vmem((128, D), F32),
            vmem((NZ_SLOTS, 8, MEM), F32),
            vmem((len(ROW_SLOTS), MEM, 128), F32),
            vmem((NZ_SLOTS, 8, MEM), F32),
            vmem((len(ROW_SLOTS), MEM, 128), F32),
            vmem((2, N_SLOTS, 2, 128), F32),
            vmem((2, 128), F32),
            vmem((64, 2, 128), F32),
            dma((3,)),
            dma((1,)),
            dma((N_SLOTS * 4,)),
            dma((1,)),
            dma((1,)),
            dma((1,)),
            dma((1,)),
        ],
        compiler_params=pltpu.CompilerParams(collective_id=0, has_side_effects=True, vmem_limit_bytes=48 << 20),
        cost_estimate=pl.CostEstimate(flops=8 << 30, bytes_accessed=8 << 20, transcendentals=0),
    )(embeddings, members, order, sizes)
    return best.reshape(MEM)


def solution(mesh):
    return jax.shard_map(
        on_device,
        mesh=mesh,
        in_specs=(P("store", None), P(), P(), P()),
        out_specs=P(("store", "grid", "row")),
        check_vma=False,
    )
```

time: 509 us -> 57.9 us (0.11)
  waiting for transfers between devices: 408 us -> 0 us
  Pallas kernels: 0 us -> 52.4 us
  other arithmetic: 30.8 us -> 0 us
  starting transfers between devices: 23.8 us -> 0 us
  between operations: 13.6 us -> 0.01 us
  matrix products: 13 us -> 0 us
  blocking collectives: 8.27 us -> 0 us
  local copies, waits for them, and re-layouts: 11 us -> 5.01 us
    ppermute x4 -> x0, waiting for transfers between devices: 358 us -> none  [from_partner(): return lax.ppermute(block, axis, route)]
    pallas_call x0 -> x1, Pallas kernels: none -> 52.4 us  [on_device(): pl.pallas_call(kernel, out_shape=jax.ShapeDtypeStruct((1, MEM), F32), in_...]
    all_gather x1 -> x0, waiting for transfers between devices: 36.6 us -> none  [on_device(): lax.all_gather(stack[None], 'grid', axis=0, tiled=True).reshape(-1, width)]
    select_n x9 -> x0, other arithmetic: 26.1 us -> none  [the longest x4 24.2 us: join_pair(): jnp.where(upper == 0, jnp.concatenate([stack, partner], axis=0), jnp.conc...]
    all_to_all x1 -> x0, starting transfers between devices: 15.1 us -> none  [on_device(): lax.all_to_all(outgoing, 'store', split_axis=0, concat_axis=0, tiled=True)]
    dot_general x1 -> x0, matrix products: 13 us -> none  [on_device(): lax.dot_general(unit, keys, (((1,), (1,)), ((), ())), preferred_element_t...]
    all_to_all x1 -> x0, waiting for transfers between devices: 13 us -> none  [on_device(): lax.all_to_all(outgoing, 'store', split_axis=0, concat_axis=0, tiled=True)]
    ppermute x4 -> x0, starting transfers between devices: 8.63 us -> none  [from_partner(): return lax.ppermute(block, axis, route)]
  transfers between devices with their start and end apart: 6 -> 0, of which waited for: 6 -> 0; matrix products, arithmetic and copies ran while one was open for 1% -> 0% of each run, Pallas kernels for 0% -> 0%
where the time goes in v1:
time: 57.9 us; the launch traced here: 57.5 us
  Pallas kernels  52.4 us (91%)
  local copies, waits for them, and re-layouts  5.01 us (9%)
    pallas_call x1, Pallas kernels, on_device(): pl.pallas_call(kernel, out_shape=jax.ShapeDtypeStruct((1, MEM), F32), in_...  52.4 us
    unnamed x9, local copies, waits for them, and re-layouts  5.01 us

profile of v1, /device:TPU:1, one launch (start us, length us, event | category | flops | bytes accessed | tf_op | source)
XLA Modules:
  0.0 57.5 jit_solution(11214128182811765499)
XLA Ops:
  0.0 0.0 copy-start
  0.0 1.9 %copy-done = bf16[2048,768]{1,0:T(8,128)(2,1)S(1)} copy-done((bf16[2048,768]{1,0:T(8,128)(2,1)S(1)}, bf16[2048,768]{1,0:T(8,128)(2,1)}, u32[]{:S(2)}) %copy-start) | copy-done | bytes 3145752
  1.9 0.0 copy-start.1
  1.9 0.9 %copy-done.1 = s32[4,16384]{1,0:T(4,128)S(1)} copy-done((s32[4,16384]{1,0:T(4,128)S(1)}, s32[4,16384]{1,0:T(4,128)}, u32[]{:S(2)}) %copy-start.1) | copy-done | bytes 262168
  2.8 0.0 copy-start.2
  2.8 0.9 %copy-done.2 = s32[4,16384]{1,0:T(4,128)S(1)} copy-done((s32[4,16384]{1,0:T(4,128)S(1)}, s32[4,16384]{1,0:T(4,128)}, u32[]{:S(2)}) %copy-start.2) | copy-done | bytes 262168
  3.8 0.0 copy-start.3
  3.8 0.7 %copy-done.3 = s32[4]{0:T(128)S(1)} copy-done((s32[4]{0:T(128)S(1)}, s32[4]{0:T(128)}, u32[]{:S(2)}) %copy-start.3) | copy-done | bytes 40
  4.4 52.4 %shard_map.46 = f32[1,256]{1,0:T(1,128)S(1)} custom-call(bf16[2048,768]{1,0:T(8,128)(2,1)S(1)} %copy-done, s32[4,16384]{1,0:T(4,128)S(1)} %copy-done.1, s32[4,16384]{1,0:T(4,128)S(1)} %copy-done.2, s32[4]{0:T(128)S(1)} %copy-done.3), custom_call_target="tpu_custom_call" | custom-call | flops 8589934592 | bytes 8388608 | tf_op jit(solution)/shard_map/pallas_call | solution.py:342
  56.9 0.6 copy.6
Async XLA Ops:
  0.0 1.9 %copy-start = (bf16[2048,768]{1,0:T(8,128)(2,1)S(1)}, bf16[2048,768]{1,0:T(8,128)(2,1)}, u32[]{:S(2)}) copy-start(bf16[2048,768]{1,0:T(8,128)(2,1)} %emb_hbm.1) | copy-start | bytes 9437188
  1.9 0.9 %copy-start.1 = (s32[4,16384]{1,0:T(4,128)S(1)}, s32[4,16384]{1,0:T(4,128)}, u32[]{:S(2)}) copy-start(s32[4,16384]{1,0:T(4,128)} %members_hbm.1) | copy-start | bytes 786436
  2.8 0.9 %copy-start.2 = (s32[4,16384]{1,0:T(4,128)S(1)}, s32[4,16384]{1,0:T(4,128)}, u32[]{:S(2)}) copy-start(s32[4,16384]{1,0:T(4,128)} %order_hbm.1) | copy-start | bytes 786436
  3.8 0.7 %copy-start.3 = (s32[4]{0:T(128)S(1)}, s32[4]{0:T(128)}, u32[]{:S(2)}) copy-start(s32[4]{0:T(128)} %sizes.1) | copy-start | bytes 52

commit v2 on v0

v2 whole, which is shorter than its diff:
```python
import jax
import jax.numpy as jnp
from jax import lax
from jax.experimental import pallas as pl
from jax.experimental.pallas import tpu as pltpu
from jax.sharding import PartitionSpec as P

AT = [(0, 0), (0, -2), (0, -1), (0, 1), (0, 2), (1, -2), (1, -1), (2, -2), (-1, -1)]
ROUTE = [(5, 5, 5, 5, 5, 5, 5, 5), (0, 0, 0, 0, 0, 0, 0, 0), (0, 0, 0, 0, 0, 0, 0, 0), (3, 3, 3, 3, 3, 3, 3, 3), (6, 6, 6, 6, 6, 6, 6, 6), (2, 2, 2, 2, 2, 2, 2, 2), (5, 5, 5, 5, 5, 5, 5, 5), (2, 2, 2, 2, 2, 2, 2, 2)]
PROGRAM = [
    ("piece", 0, 4),
    ("piece", 2, 0),
    ("piece", 3, 0),
    ("piece", 0, 5),
    ("piece", 2, 3),
    ("piece", 3, 3),
    ("piece", 0, 6),
    ("piece", 2, 2),
    ("piece", 3, 2),
    ("piece", 0, 7),
    ("piece", 2, 1),
    ("piece", 3, 1),
    ("piece", 6, 0),
    ("piece", 8, 0),
    ("piece", 2, 4),
    ("piece", 4, 0),
    ("piece", 6, 3),
    ("piece", 8, 3),
    ("piece", 2, 5),
    ("piece", 4, 3),
    ("piece", 6, 2),
    ("piece", 8, 2),
    ("piece", 2, 6),
    ("piece", 3, 6),
    ("twin", 0, 0),
    ("twin", 0, 1),
    ("products", ((0, 0, False),)),
    ("piece", 6, 1),
    ("piece", 8, 1),
    ("piece", 2, 7),
    ("piece", 4, 2),
    ("products", ((2, 0, True),)),
    ("piece", 6, 4),
    ("piece", 8, 4),
    ("piece", 4, 1),
    ("piece", 5, 0),
    ("piece", 6, 5),
    ("piece", 8, 5),
    ("piece", 3, 4),
    ("piece", 5, 3),
    ("piece", 6, 6),
    ("piece", 8, 6),
    ("piece", 4, 6),
    ("piece", 5, 2),
    ("piece", 6, 7),
    ("piece", 8, 7),
    ("products", ((6, 0, True),)),
    ("piece", 3, 5),
    ("piece", 5, 1),
    ("twin", 2, 0),
    ("twin", 2, 1),
    ("products", ((6, 2, True),)),
    ("piece", 1, 0),
    ("piece", 7, 0),
    ("known",),
    ("piece", 3, 7),
    ("piece", 5, 4),
    ("products", ((8, 0, True),)),
    ("piece", 1, 3),
    ("piece", 7, 3),
    ("products", ((3, 2, True),)),
    ("piece", 4, 4),
    ("piece", 5, 5),
    ("piece", 1, 2),
    ("piece", 7, 2),
    ("twin", 8, 0),
    ("twin", 8, 1),
    ("products", ((3, 8, True),)),
    ("piece", 5, 6),
    ("products", ((6, 8, False),)),
    ("piece", 1, 1),
    ("piece", 4, 5),
    ("piece", 7, 1),
    ("piece", 5, 7),
    ("twin", 3, 0),
    ("twin", 3, 1),
    ("products", ((6, 3, True),)),
    ("piece", 1, 4),
    ("piece", 4, 7),
    ("piece", 7, 4),
    ("products", ((5, 3, True), (5, 8, True))),
    ("piece", 1, 5),
    ("piece", 7, 5),
    ("products", ((4, 2, True), (4, 8, True))),
    ("piece", 1, 6),
    ("piece", 7, 6),
    ("twin", 5, 0),
    ("twin", 5, 1),
    ("products", ((4, 5, True),)),
    ("piece", 1, 7),
    ("piece", 7, 7),
    ("twin", 4, 0),
    ("twin", 4, 1),
    ("products", ((1, 4, False), (7, 0, True), (7, 3, True), (7, 4, False))),
]
D = 768
MEM = 256
BLOCKS = 64
PIECES = len(ROUTE[0])
HALF = PIECES // 2
ROWS = MEM // PIECES
NEVER = float(1 << 20)
MESH = pl.DeviceIdType.MESH
F32 = jnp.float32
N_SLOTS = len(AT)
PRODUCTS = [one for step in PROGRAM if step[0] == "products" for one in step[1]]
LEFT = sorted({one[0] for one in PRODUCTS})
RIGHT = sorted({one[1] for one in PRODUCTS})
BASE = [s + sum(r < s for r in RIGHT) for s in range(N_SLOTS)]
N_HELD = N_SLOTS + len(RIGHT)
PARTS = [(AT[s], 0) for s in LEFT] + [(AT[s], other) for s in RIGHT for other in (0, 1)]
STEPS = {tuple((a - b) for a, b in zip(AT[s], AT[ROUTE[s - 1][q]])) for s in range(1, N_SLOTS) for q in range(PIECES)}
N_SENT = PIECES * (N_SLOTS - 1) + PIECES * len(RIGHT) + HALF


def coordinates():
    store = lax.axis_index("store")
    return store // 16, (store // 8) % 2, store % 8, lax.axis_index("grid"), lax.axis_index("row")


def device(x, y_hi, z, core, y_lo):
    return (x * 16 + y_hi * 8 + z, core, y_lo)


def spread(row):
    return jnp.transpose(jnp.broadcast_to(row, (128, 128)))


def lookup(n, values):
    if len(set(values)) == 1:
        return values[0]
    found = jnp.int32(values[0])
    for k in range(1, len(values)):
        if values[k] != values[0]:
            found = jnp.where(n == k, jnp.int32(values[k]), found)
    return found


def kernel(emb_hbm, members_hbm, order_hbm, sizes_hbm, out, sizes, emb, members, order, table, held, give, vec, col_ord, row_ord, col_best, row_best, lines, tell, got, swap, load_sem, send_sem, recv_sem, twin_sem, route_send, route_recv, known):
    x, y_hi, z, core, y_lo = coordinates()
    y = y_hi * 2 + y_lo
    store = x * 16 + y_hi * 8 + z

    def at(dx, dz, other=0, across=False):
        side = core if other == 0 else 1 - core
        if across:
            return device((x + dx + 4) % 4, 1 - y_hi, (z + dz + 8) % 8, side, 1 - y_lo)
        return device((x + dx + 4) % 4, y_hi, (z + dz + 8) % 8, side, y_lo)

    near = sorted({((sign * dx) % 4, (sign * dz) % 8) for dx, dz in STEPS for sign in (1, -1)})
    greet = [at(dx, dz) for dx, dz in near] + [at(0, 0, 0, True), at(0, 0, 1)]
    greet += [device(x, y_hi, z, core, 1 - y_lo), device(x, 1 - y_hi, z, core, y_lo)]
    barrier = pltpu.get_barrier_semaphore()
    for one in greet:
        pl.semaphore_signal(barrier, inc=1, device_id=one, device_id_type=MESH)

    loads = [
        pltpu.make_async_copy(members_hbm, members, load_sem.at[0]),
        pltpu.make_async_copy(order_hbm, order, load_sem.at[1]),
        pltpu.make_async_copy(emb_hbm, emb, load_sem.at[2]),
        pltpu.make_async_copy(sizes_hbm, sizes, load_sem.at[3]),
    ]
    for one in loads:
        one.start()
    loads[0].wait()

    def lay(ref, cluster, where):
        for b in range(BLOCKS):
            line = ref[pl.ds(cluster, 1), b * MEM : (b + 1) * MEM]
            table[where, b : b + 1, :] = line
            table[where, BLOCKS + b : BLOCKS + b + 1, :] = line

    lay(members, y, 0)
    lay(members, 3 - y, 1)
    ids = jnp.transpose(table[0])
    ids_partner = jnp.transpose(table[1])
    upper = lax.broadcasted_iota(jnp.int32, (1, 128), 1) // BLOCKS
    before = (
        lax.broadcasted_iota(jnp.int32, (MEM, MEM), 1) < lax.broadcasted_iota(jnp.int32, (MEM, MEM), 0)
    ).astype(jnp.bfloat16)

    def ranks(local):
        inside = (local >= 0) & (local < 2048)
        count = jnp.dot(before, jnp.where(inside, 1.0, 0.0).astype(jnp.bfloat16), preferred_element_type=F32)
        return jnp.where(inside, count, -1.0)

    def pick(rank, side, values):
        wanted = (2 * side + upper).astype(F32)
        return jnp.sum(jnp.where(rank == wanted, values, 0.0), axis=0, keepdims=True)

    chosen = []
    for table_ids in (ids_partner, ids):
        local = table_ids - store * 2048
        chosen.append(spread(pick(ranks(local), core, local.astype(F32))).astype(jnp.int32))
    loads[2].wait()
    lane = lax.broadcasted_iota(jnp.int32, (128, 128), 1)
    for half in range(2):
        onehot = jnp.concatenate([jnp.where(chosen[half] == lane + 128 * j, 1.0, 0.0).astype(jnp.bfloat16) for j in range(16)], axis=1)
        for n in range(3):
            vec[:, n * 256 : (n + 1) * 256] = jnp.dot(onehot, emb[:, n * 256 : (n + 1) * 256], preferred_element_type=F32)
        vector = vec[...]
        scale = lax.rsqrt(jnp.sum(vector * vector, axis=1, keepdims=True) + 1e-06)
        unit = (vector * scale).astype(jnp.bfloat16).reshape(HALF, ROWS, D)
        if half == 0:
            give[...] = unit
        else:
            held[pl.ds(y_hi * HALF, HALF)] = unit

    pl.semaphore_wait(barrier, len(greet))

    def side_of(half):
        return y_hi if half == 0 else 1 - y_hi

    def piece(slot, q):
        return BASE[slot] * PIECES + side_of(q // HALF) * HALF + q % HALF

    def push(src, dst, sem, to):
        pltpu.make_async_remote_copy(src, dst, send_sem.at[0], sem, device_id=to, device_id_type=MESH).start()

    def landed(ref, sem):
        pltpu.make_async_remote_copy(ref, ref, send_sem.at[0], sem, device_id=at(0, 0, 1), device_id_type=MESH).wait_recv()

    def forward(slot, q):
        for s in range(1, N_SLOTS):
            if ROUTE[s - 1][q] == slot:
                push(held.at[piece(slot, q)], held.at[piece(s, q)], recv_sem.at[s * PIECES + q], at(AT[slot][0] - AT[s][0], AT[slot][1] - AT[s][1]))

    def twin(slot, half):
        if slot in RIGHT:
            where = BASE[slot] * PIECES + side_of(half) * HALF
            push(held.at[pl.ds(where, HALF)], held.at[pl.ds(where + PIECES, HALF)], twin_sem.at[slot * 2 + half], at(0, 0, 1))

    for q in range(HALF):
        push(give.at[q], held.at[y_hi * HALF + q], recv_sem.at[HALF + q], at(0, 0, 0, True))
        forward(0, q)
    twin(0, 0)

    loads[1].wait()
    loads[3].wait()
    lay(order, y, 2)
    slot = lax.broadcasted_iota(jnp.int32, (MEM, 128), 0) + MEM * (lax.broadcasted_iota(jnp.int32, (MEM, 128), 1) % BLOCKS)
    rank_of = jnp.where(slot < sizes[y], jnp.transpose(table[2]).astype(F32), NEVER)
    for s in range(N_SLOTS):
        for hi in range(2):
            shard = ((x + AT[s][0] + 4) % 4) * 16 + hi * 8 + (z + AT[s][1] + 8) % 8
            rank = ranks(ids - shard * 2048)
            line = pick(rank, core, rank_of)
            if s in LEFT:
                row_ord[LEFT.index(s), hi * 128 : (hi + 1) * 128, :] = spread(line)
            if s in RIGHT:
                r = RIGHT.index(s)
                col_ord[r, :, hi * 128 : (hi + 1) * 128] = jnp.broadcast_to(line, (8, 128))
                line = pick(rank, 1 - core, rank_of)
                col_ord[r, :, 256 + hi * 128 : 256 + (hi + 1) * 128] = jnp.broadcast_to(line, (8, 128))
    col_best[...] = jnp.full(col_best.shape, -1.0, F32)
    row_best[...] = jnp.full(row_best.shape, -1.0, F32)

    def products(group):
        def one(n, carry):
            left = lookup(n, [LEFT.index(a) for a, b, full in group])
            left_at = lookup(n, [BASE[a] * PIECES for a, b, full in group])
            right = lookup(n, [RIGHT.index(b) for a, b, full in group])
            right_at = lookup(n, [BASE[b] * PIECES for a, b, full in group])
            column = lookup(n, [RIGHT.index(b) if full else len(RIGHT) for a, b, full in group])
            a = held[pl.ds(left_at, PIECES)].reshape(MEM, D)
            b = held[pl.ds(right_at, 2 * PIECES)].reshape(2 * MEM, D)
            score = lax.dot_general(a, b, (((1,), (1,)), ((), ())), preferred_element_type=F32)
            own = row_ord[left]
            best = row_best[left]
            for part in range(4):
                lanes = slice(part * 128, (part + 1) * 128)
                mine = score[:, lanes]
                earlier = col_ord[right, 0:1, lanes] < own
                best = jnp.maximum(best, jnp.where(earlier, mine, -1.0))
                later = jnp.max(jnp.where(earlier, -1.0, mine).reshape(32, 8, 128), axis=0)
                col_best[column, :, lanes] = jnp.maximum(col_best[column, :, lanes], later)
            row_best[left] = best
            return carry

        if len(group) == 1:
            one(0, 0)
        else:
            lax.fori_loop(0, len(group), one, 0)

    for step in PROGRAM:
        if step[0] == "piece":
            s, q = step[1:]
            landed(held.at[piece(s, q)], recv_sem.at[s * PIECES + q])
            forward(s, q)
            half = {("piece", s, r) for r in range(PIECES) if r // HALF == q // HALF}
            if half <= set(PROGRAM[: PROGRAM.index(step) + 1]):
                twin(s, q // HALF)
        elif step[0] == "known":
            for s in range(N_SLOTS):
                for other in (0, 1):
                    if s > 0 or other > 0:
                        pl.semaphore_signal(known, inc=1, device_id=at(AT[s][0], AT[s][1], other), device_id_type=MESH)
        elif step[0] == "twin":
            s, half = step[1:]
            landed(held.at[pl.ds(BASE[s] * PIECES + PIECES + side_of(half) * HALF, HALF)], twin_sem.at[s * 2 + half])
        else:
            products(step[1])

    for p in range(len(PARTS)):
        for hi in range(2):
            if p < len(LEFT):
                line = jnp.max(jnp.transpose(row_best[p, hi * 128 : (hi + 1) * 128, :]), axis=0, keepdims=True)
            else:
                r, other = (p - len(LEFT)) // 2, (p - len(LEFT)) % 2
                line = jnp.max(col_best[r, :, other * 256 + hi * 128 : other * 256 + (hi + 1) * 128], axis=0, keepdims=True)
            lines[p * 2 + hi : p * 2 + hi + 1, :] = line
    turned = jnp.transpose(lines[...])
    tell[:, 0, :] = turned[:BLOCKS]
    tell[:, 1, :] = turned[BLOCKS:]

    pl.semaphore_wait(known, 2 * N_SLOTS - 1)

    sender = (x * 8 + z) * 2 + core
    home = (y_hi * 8 + z) * 4 + core * 2 + y_lo

    def route(n, carry):
        b = lax.rem(home + n, 64)
        pltpu.make_async_remote_copy(
            tell.at[b],
            got.at[sender],
            route_send.at[0],
            route_recv.at[0],
            device_id=(y * 16 + b // 4, (b // 2) % 2, b % 2),
            device_id_type=MESH,
        ).start()
        return carry

    @pl.when(x == y)
    def _():
        pltpu.make_async_copy(tell.at[home], got.at[sender], route_recv.at[0]).start()

    @pl.when(x != y)
    def _():
        route(0, 0)

    lax.fori_loop(1, 64, route, 0)

    block = home
    own_ids = members[pl.ds(x, 1), pl.ds(pl.multiple_of(block * MEM, MEM), MEM)]
    shard = own_ids // 2048
    shard_rows = jnp.concatenate([spread(shard[:, :128].astype(F32)), spread(shard[:, 128:].astype(F32))], axis=0)
    shard_rows = jnp.concatenate([shard_rows, shard_rows], axis=1)
    same = (shard_rows == shard.astype(F32)) & (
        lax.broadcasted_iota(jnp.int32, (MEM, MEM), 0) < lax.broadcasted_iota(jnp.int32, (MEM, MEM), 1)
    )
    rank = jnp.sum(jnp.where(same, 1.0, 0.0), axis=0, keepdims=True).astype(jnp.int32)
    from_sender = ((shard // 16) * 8 + shard % 8) * 2 + rank // 2
    from_place = (rank % 2) * 2 + (shard // 8) % 2
    from_which = from_sender * 4 + from_place
    slots = block * MEM + lax.broadcasted_iota(jnp.int32, (1, MEM), 1)
    in_use = slots < sizes[x]
    lane_z = lax.broadcasted_iota(jnp.int32, (4, 128), 1) % 16
    senders = lax.broadcasted_iota(jnp.int32, (64, MEM), 0)

    pltpu.make_async_remote_copy(got, got, route_send.at[0], route_recv.at[0], device_id=at(0, 0, 1), device_id_type=MESH).wait_recv()
    for rr in range(2):
        heard = got[:, rr, :]
        swap[rr] = jnp.transpose(jnp.concatenate([heard, heard], axis=0))
    value = jnp.full((4, 128), -1.0, F32)
    for p in range(len(PARTS)):
        (dx, dz), other = PARTS[p]
        rows = jnp.concatenate([swap[0, 2 * p : 2 * p + 2, :], swap[1, 2 * p : 2 * p + 2, :]], axis=0)
        if dx % 4 or dz % 8:
            turn = 16 * (dx % 4) + 2 * (dz % 8)
            moved = pltpu.roll(rows, turn, 1)
            if dz % 8:
                moved = jnp.where(lane_z >= 2 * (dz % 8), moved, pltpu.roll(rows, (turn - 16) % 128, 1))
            rows = moved
        if other:
            rows = jnp.where(lane_z % 2 == 0, pltpu.roll(rows, 127, 1), pltpu.roll(rows, 1, 1))
        value = jnp.maximum(value, rows)
    final = jnp.zeros((1, MEM), F32)
    for place in range(4):
        column = spread(value[place : place + 1, :])[:64]
        column = jnp.concatenate([column, column], axis=1)
        here = from_which == senders * 4 + place
        final = final + jnp.sum(jnp.where(here, column, 0.0), axis=0, keepdims=True)
    out[...] = jnp.where(in_use, final, 0.0)

    sent = held.at[pl.ds(0, N_SENT)]
    pltpu.make_async_remote_copy(sent, sent, send_sem.at[0], recv_sem.at[0], device_id=at(0, 0, 1), device_id_type=MESH).wait_send()

    @pl.when(x == y)
    def _():
        fewer = got.at[pl.ds(0, 63)]
        pltpu.make_async_remote_copy(fewer, fewer, route_send.at[0], route_recv.at[0], device_id=at(0, 0, 1), device_id_type=MESH).wait_send()

    @pl.when(x != y)
    def _():
        pltpu.make_async_remote_copy(got, got, route_send.at[0], route_recv.at[0], device_id=at(0, 0, 1), device_id_type=MESH).wait_send()


def on_device(embeddings, members, order, sizes):
    vmem = pltpu.VMEM
    dma = pltpu.SemaphoreType.DMA
    best = pl.pallas_call(
        kernel,
        out_shape=jax.ShapeDtypeStruct((1, MEM), F32),
        in_specs=[pl.BlockSpec(memory_space=pltpu.HBM)] * 4,
        out_specs=pl.BlockSpec(memory_space=pltpu.VMEM),
        scratch_shapes=[
            pltpu.SMEM((4,), jnp.int32),
            vmem((2048, D), jnp.bfloat16),
            vmem((4, 16384), jnp.int32),
            vmem((4, 16384), jnp.int32),
            vmem((3, 128, MEM), jnp.int32),
            vmem((max(N_HELD * PIECES, N_SENT), ROWS, D), jnp.bfloat16),
            vmem((HALF, ROWS, D), jnp.bfloat16),
            vmem((128, D), F32),
            vmem((len(RIGHT), 8, 512), F32),
            vmem((len(LEFT), MEM, 128), F32),
            vmem((len(RIGHT) + 1, 8, 512), F32),
            vmem((len(LEFT), MEM, 128), F32),
            vmem((128, 128), F32),
            vmem((64, 2, 128), F32),
            vmem((64, 2, 128), F32),
            vmem((2, 128, 128), F32),
            dma((4,)),
            dma((1,)),
            dma((N_SLOTS * PIECES,)),
            dma((N_SLOTS * 2,)),
            dma((1,)),
            dma((1,)),
            pltpu.SemaphoreType.REGULAR,
        ],
        compiler_params=pltpu.CompilerParams(collective_id=0, has_side_effects=True, vmem_limit_bytes=64 << 20),
        cost_estimate=pl.CostEstimate(flops=8 << 30, bytes_accessed=8 << 20, transcendentals=0),
    )(embeddings, members, order, sizes)
    return best.reshape(MEM)


def solution(mesh):
    return jax.shard_map(
        on_device,
        mesh=mesh,
        in_specs=(P("store", None), P(), P(), P()),
        out_specs=P(("store", "grid", "row")),
        check_vma=False,
    )
```

time: 509 us -> 48.2 us (0.09)
  waiting for transfers between devices: 408 us -> 0 us
  Pallas kernels: 0 us -> 46.8 us
  other arithmetic: 30.8 us -> 0 us
  starting transfers between devices: 23.8 us -> 0 us
  between operations: 13.6 us -> 0.01 us
  matrix products: 13 us -> 0 us
  local copies, waits for them, and re-layouts: 11 us -> 1.24 us
  blocking collectives: 8.27 us -> 0 us
    ppermute x4 -> x0, waiting for transfers between devices: 358 us -> none  [from_partner(): return lax.ppermute(block, axis, route)]
    pallas_call x0 -> x1, Pallas kernels: none -> 46.8 us  [on_device(): pl.pallas_call(kernel, out_shape=jax.ShapeDtypeStruct((1, MEM), F32), in_...]
    all_gather x1 -> x0, waiting for transfers between devices: 36.6 us -> none  [on_device(): lax.all_gather(stack[None], 'grid', axis=0, tiled=True).reshape(-1, width)]
    select_n x9 -> x0, other arithmetic: 26.1 us -> none  [the longest x4 24.2 us: join_pair(): jnp.where(upper == 0, jnp.concatenate([stack, partner], axis=0), jnp.conc...]
    all_to_all x1 -> x0, starting transfers between devices: 15.1 us -> none  [on_device(): lax.all_to_all(outgoing, 'store', split_axis=0, concat_axis=0, tiled=True)]
    dot_general x1 -> x0, matrix products: 13 us -> none  [on_device(): lax.dot_general(unit, keys, (((1,), (1,)), ((), ())), preferred_element_t...]
    all_to_all x1 -> x0, waiting for transfers between devices: 13 us -> none  [on_device(): lax.all_to_all(outgoing, 'store', split_axis=0, concat_axis=0, tiled=True)]
    ppermute x4 -> x0, starting transfers between devices: 8.63 us -> none  [from_partner(): return lax.ppermute(block, axis, route)]
  transfers between devices with their start and end apart: 6 -> 0, of which waited for: 6 -> 0; matrix products, arithmetic and copies ran while one was open for 1% -> 0% of each run, Pallas kernels for 0% -> 0%
where the time goes in v2:
time: 48.2 us; the launch traced here: 48.1 us
  Pallas kernels  46.8 us (97%)
  local copies, waits for them, and re-layouts  1.24 us (3%)
    pallas_call x1, Pallas kernels, on_device(): pl.pallas_call(kernel, out_shape=jax.ShapeDtypeStruct((1, MEM), F32), in_...  46.8 us
    unnamed x1, local copies, waits for them, and re-layouts  1.24 us

profile of v2, /device:TPU:1, one launch (start us, length us, event | category | flops | bytes accessed | tf_op | source)
XLA Modules:
  0.0 48.1 jit_solution(5700306500212697274)
XLA Ops:
  0.0 46.8 %shard_map.46 = f32[1,256]{1,0:T(1,128)} custom-call(bf16[2048,768]{1,0:T(8,128)(2,1)} %emb_hbm.1, s32[4,16384]{1,0:T(4,128)} %members_hbm.1, s32[4,16384]{1,0:T(4,128)} %order_hbm.1, s32[4]{0:T(128)} %sizes_hbm.1), custom_call_target="tpu_custom_call" | custom-call | flops 8589934592 | bytes 8388608 | tf_op jit(solution)/shard_map/pallas_call | solution.py:411
  46.9 1.2 %copy.6 = f32[256]{0:T(256)} copy(f32[256]{0:T(256)} %bitcast.1) | data formatting | bytes 2048

commit v3 on v2

--- a/solution.py
+++ b/solution.py
@@ -111,6 +111,7 @@
 ROWS = MEM // PIECES
 NEVER = float(1 << 20)
 MESH = pl.DeviceIdType.MESH
+FAR_FIRST = (4, 3, 5, 2, 6, 1, 7, 0)
 F32 = jnp.float32
 N_SLOTS = len(AT)
 PRODUCTS = [one for step in PROGRAM if step[0] == "products" for one in step[1]]
@@ -290,7 +291,7 @@
         if len(group) == 1:
             one(0, 0)
         else:
-            lax.fori_loop(0, len(group), one, 0)
+            lax.fori_loop(0, len(group), one, 0, unroll=True)
 
     for step in PROGRAM:
         if step[0] == "piece":
@@ -329,26 +330,37 @@
     home = (y_hi * 8 + z) * 4 + core * 2 + y_lo
 
     def route(n, carry):
-        b = lax.rem(home + n, 64)
-        pltpu.make_async_remote_copy(
-            tell.at[b],
-            got.at[sender],
-            route_send.at[0],
-            route_recv.at[0],
-            device_id=(y * 16 + b // 4, (b // 2) % 2, b % 2),
-            device_id_type=MESH,
-        ).start()
+        to_z = lax.rem(z + lookup(n, FAR_FIRST), 8)
+        for over, low in ((1, 0), (1, 1), (0, 1), (0, 0)):
+            to_hi = 1 - y_hi if over else y_hi
+            to_lo = 1 - y_lo if low else y_lo
+            for twin_core in (1, 0):
+                to_core = 1 - core if twin_core else core
+                store_there = to_hi * 8 + to_z
+
+                def remote():
+                    pltpu.make_async_remote_copy(
+                        tell.at[store_there * 4 + to_core * 2 + to_lo],
+                        got.at[sender],
+                        route_send.at[0],
+                        route_recv.at[0],
+                        device_id=(y * 16 + store_there, to_core, to_lo),
+                        device_id_type=MESH,
+                    ).start()
+
+                if over or low or twin_core:
+                    remote()
+                else:
+                    here = (x == y) & (n == len(FAR_FIRST) - 1)
+                    pl.when(jnp.logical_not(here))(remote)
+
+                    @pl.when(here)
+                    def _():
+                        pltpu.make_async_copy(tell.at[home], got.at[sender], route_recv.at[0]).start()
+
         return carry
 
-    @pl.when(x == y)
-    def _():
-        pltpu.make_async_copy(tell.at[home], got.at[sender], route_recv.at[0]).start()
-
-    @pl.when(x != y)
-    def _():
-        route(0, 0)
-
-    lax.fori_loop(1, 64, route, 0)
+    lax.fori_loop(0, len(FAR_FIRST), route, 0)
 
     block = home
     own_ids = members[pl.ds(x, 1), pl.ds(pl.multiple_of(block * MEM, MEM), MEM)]
@@ -438,9 +450,9 @@
             dma((1,)),
             pltpu.SemaphoreType.REGULAR,
         ],
-        compiler_params=pltpu.CompilerParams(collective_id=0, has_side_effects=True, vmem_limit_bytes=64 << 20),
+        compiler_params=pltpu.CompilerParams(collective_id=0, has_side_effects=True, vmem_limit_bytes=48 << 20),
         cost_estimate=pl.CostEstimate(flops=8 << 30, bytes_accessed=8 << 20, transcendentals=0),
-    )(embeddings, members, order, sizes)
+    )(*[pltpu.with_memory_space_constraint(one, pltpu.HBM) for one in (embeddings, members, order, sizes)])
     return best.reshape(MEM)
 
 

time: 48.2 us -> 44.5 us (0.923)
  Pallas kernels: 46.8 us -> 43.9 us
  local copies, waits for them, and re-layouts: 1.24 us -> 0.56 us
    pallas_call x1, Pallas kernels: 46.8 us -> 43.9 us  [on_device(): pl.pallas_call(kernel, out_shape=jax.ShapeDtypeStruct((1, MEM), F32), in_...]
    unnamed x1, local copies, waits for them, and re-layouts: 1.24 us -> 0.56 us
where the time goes in v3:
time: 44.5 us
  Pallas kernels  43.9 us (99%)
  local copies, waits for them, and re-layouts  0.56 us (1%)
    pallas_call x1, Pallas kernels, on_device(): pl.pallas_call(kernel, out_shape=jax.ShapeDtypeStruct((1, MEM), F32), in_...  43.9 us

profile of v3, /device:TPU:1, one launch (start us, length us, event | category | flops | bytes accessed | tf_op | source)
XLA Modules:
  0.0 44.5 jit_solution(14711786714713128349)
XLA Ops:
  0.0 43.9 %shard_map.46 = f32[1,256]{1,0:T(1,128)S(1)} custom-call(bf16[2048,768]{1,0:T(8,128)(2,1)} %emb_hbm.1, s32[4,16384]{1,0:T(4,128)} %members_hbm.1, s32[4,16384]{1,0:T(4,128)} %order_hbm.1, s32[4]{0:T(128)} %sizes_hbm.1), custom_call_target="tpu_custom_call" | custom-call | flops 8589934592 | bytes 8388608 | tf_op jit(solution)/shard_map/pallas_call | solution.py:423
  43.9 0.6 %copy.6 = f32[256]{0:T(256)} copy(f32[256]{0:T(256)S(1)} %bitcast.1) | data formatting | bytes 2048

commit v4 on v3

--- a/solution.py
+++ b/solution.py
@@ -5,103 +5,162 @@
 from jax.experimental.pallas import tpu as pltpu
 from jax.sharding import PartitionSpec as P
 
-AT = [(0, 0), (0, -2), (0, -1), (0, 1), (0, 2), (1, -2), (1, -1), (2, -2), (-1, -1)]
-ROUTE = [(5, 5, 5, 5, 5, 5, 5, 5), (0, 0, 0, 0, 0, 0, 0, 0), (0, 0, 0, 0, 0, 0, 0, 0), (3, 3, 3, 3, 3, 3, 3, 3), (6, 6, 6, 6, 6, 6, 6, 6), (2, 2, 2, 2, 2, 2, 2, 2), (5, 5, 5, 5, 5, 5, 5, 5), (2, 2, 2, 2, 2, 2, 2, 2)]
+AT = [(0, 0), (0, -2), (0, -1), (0, 1), (0, 2), (1, 1), (2, 2), (-1, 1), (-1, 2)]
+ROUTE = [(2, 2, 2, 2, 2, 2, 2, 2), (0, 0, 0, 0, 0, 0, 0, 0), (0, 0, 0, 0, 0, 0, 0, 0), (8, 8, 8, 8, 8, 8, 3, 8), (3, 3, 3, 3, 3, 3, 3, 3), (8, 8, 8, 8, 8, 8, 8, 8), (3, 3, 3, 3, 3, 3, 3, 3), (7, 7, 7, 7, 7, 7, 7, 7)]
 PROGRAM = [
+    ("send", 2, 1),
+    ("send", 3, 1),
+    ("send", 2, 3),
+    ("send", 3, 3),
+    ("send", 2, 0),
+    ("send", 3, 0),
+    ("send", 2, 2),
+    ("send", 3, 2),
     ("piece", 0, 4),
-    ("piece", 2, 0),
-    ("piece", 3, 0),
+    ("piece", 2, 1),
+    ("piece", 3, 1),
+    ("send", 1, 1),
+    ("send", 3, 4),
+    ("send", 5, 1),
+    ("send", 7, 1),
+    ("send", 2, 4),
     ("piece", 0, 5),
     ("piece", 2, 3),
     ("piece", 3, 3),
+    ("send", 1, 3),
+    ("send", 3, 5),
+    ("send", 5, 3),
+    ("send", 7, 3),
     ("piece", 0, 6),
+    ("piece", 2, 0),
+    ("piece", 3, 0),
+    ("send", 3, 6),
+    ("send", 5, 0),
+    ("send", 7, 0),
+    ("piece", 0, 7),
     ("piece", 2, 2),
     ("piece", 3, 2),
-    ("piece", 0, 7),
-    ("piece", 2, 1),
-    ("piece", 3, 1),
-    ("piece", 6, 0),
-    ("piece", 8, 0),
+    ("send", 2, 7),
+    ("send", 3, 7),
+    ("send", 5, 2),
+    ("send", 7, 2),
+    ("send", 2, 5),
+    ("piece", 5, 1),
+    ("piece", 7, 1),
+    ("send", 8, 1),
+    ("piece", 1, 1),
+    ("piece", 3, 4),
+    ("send", 5, 4),
+    ("send", 7, 4),
+    ("piece", 5, 3),
+    ("piece", 7, 3),
+    ("send", 8, 3),
     ("piece", 2, 4),
-    ("piece", 4, 0),
-    ("piece", 6, 3),
-    ("piece", 8, 3),
-    ("piece", 2, 5),
-    ("piece", 4, 3),
-    ("piece", 6, 2),
-    ("piece", 8, 2),
-    ("piece", 2, 6),
-    ("piece", 3, 6),
+    ("piece", 3, 5),
+    ("send", 1, 4),
+    ("send", 5, 5),
+    ("send", 7, 5),
+    ("send", 1, 0),
+    ("piece", 5, 0),
+    ("piece", 7, 0),
+    ("send", 8, 0),
     ("twin", 0, 0),
     ("twin", 0, 1),
     ("products", ((0, 0, False),)),
+    ("piece", 1, 3),
+    ("piece", 3, 6),
+    ("send", 5, 6),
+    ("send", 7, 6),
+    ("piece", 5, 2),
+    ("piece", 7, 2),
+    ("piece", 2, 7),
+    ("piece", 3, 7),
+    ("send", 1, 7),
+    ("send", 5, 7),
+    ("send", 7, 7),
+    ("send", 2, 6),
+    ("piece", 5, 4),
+    ("piece", 7, 4),
+    ("send", 8, 4),
+    ("send", 8, 2),
+    ("products", ((3, 0, True),)),
+    ("send", 1, 2),
+    ("piece", 2, 5),
+    ("piece", 8, 1),
+    ("send", 4, 1),
+    ("send", 6, 1),
+    ("piece", 5, 5),
+    ("piece", 7, 5),
+    ("send", 8, 5),
+    ("send", 1, 5),
+    ("piece", 1, 4),
+    ("piece", 8, 3),
+    ("send", 4, 3),
+    ("send", 6, 3),
+    ("piece", 5, 6),
+    ("piece", 7, 6),
+    ("piece", 1, 0),
+    ("piece", 8, 0),
+    ("send", 4, 0),
+    ("send", 6, 0),
+    ("piece", 5, 7),
+    ("piece", 7, 7),
+    ("send", 8, 7),
+    ("send", 8, 6),
+    ("products", ((5, 0, True),)),
+    ("send", 4, 6),
+    ("piece", 1, 7),
+    ("piece", 8, 4),
+    ("send", 4, 4),
+    ("send", 6, 4),
+    ("piece", 4, 1),
     ("piece", 6, 1),
-    ("piece", 8, 1),
-    ("piece", 2, 7),
-    ("piece", 4, 2),
-    ("products", ((2, 0, True),)),
+    ("known",),
+    ("products", ((7, 0, True),)),
+    ("piece", 2, 6),
+    ("piece", 8, 2),
+    ("send", 1, 6),
+    ("send", 4, 2),
+    ("send", 6, 2),
+    ("piece", 4, 3),
+    ("piece", 6, 3),
+    ("twin", 5, 0),
+    ("twin", 5, 1),
+    ("products", ((2, 5, True),)),
+    ("piece", 1, 2),
+    ("piece", 8, 5),
+    ("send", 4, 5),
+    ("send", 6, 5),
+    ("piece", 4, 0),
+    ("piece", 6, 0),
+    ("products", ((3, 5, True), (7, 5, False))),
+    ("piece", 1, 5),
+    ("piece", 8, 7),
+    ("send", 4, 7),
+    ("send", 6, 7),
+    ("piece", 4, 4),
     ("piece", 6, 4),
-    ("piece", 8, 4),
-    ("piece", 4, 1),
-    ("piece", 5, 0),
-    ("piece", 6, 5),
-    ("piece", 8, 5),
-    ("piece", 3, 4),
-    ("piece", 5, 3),
-    ("piece", 6, 6),
-    ("piece", 8, 6),
-    ("piece", 4, 6),
-    ("piece", 5, 2),
-    ("piece", 6, 7),
-    ("piece", 8, 7),
-    ("products", ((6, 0, True),)),
-    ("piece", 3, 5),
-    ("piece", 5, 1),
     ("twin", 2, 0),
     ("twin", 2, 1),
-    ("products", ((6, 2, True),)),
-    ("piece", 1, 0),
-    ("piece", 7, 0),
-    ("known",),
-    ("piece", 3, 7),
-    ("piece", 5, 4),
-    ("products", ((8, 0, True),)),
-    ("piece", 1, 3),
-    ("piece", 7, 3),
-    ("products", ((3, 2, True),)),
-    ("piece", 4, 4),
-    ("piece", 5, 5),
-    ("piece", 1, 2),
-    ("piece", 7, 2),
-    ("twin", 8, 0),
-    ("twin", 8, 1),
-    ("products", ((3, 8, True),)),
-    ("piece", 5, 6),
-    ("products", ((6, 8, False),)),
-    ("piece", 1, 1),
+    ("products", ((3, 2, True), (7, 2, True))),
+    ("piece", 8, 6),
+    ("send", 6, 6),
+    ("piece", 1, 6),
+    ("piece", 4, 2),
+    ("piece", 6, 2),
+    ("products", ((8, 2, True), (8, 5, True))),
+    ("piece", 4, 6),
     ("piece", 4, 5),
-    ("piece", 7, 1),
-    ("piece", 5, 7),
-    ("twin", 3, 0),
-    ("twin", 3, 1),
-    ("products", ((6, 3, True),)),
-    ("piece", 1, 4),
+    ("piece", 6, 5),
+    ("products", ((1, 5, True),)),
     ("piece", 4, 7),
-    ("piece", 7, 4),
-    ("products", ((5, 3, True), (5, 8, True))),
-    ("piece", 1, 5),
-    ("piece", 7, 5),
-    ("products", ((4, 2, True), (4, 8, True))),
-    ("piece", 1, 6),
-    ("piece", 7, 6),
-    ("twin", 5, 0),
-    ("twin", 5, 1),
-    ("products", ((4, 5, True),)),
-    ("piece", 1, 7),
-    ("piece", 7, 7),
-    ("twin", 4, 0),
-    ("twin", 4, 1),
-    ("products", ((1, 4, False), (7, 0, True), (7, 3, True), (7, 4, False))),
+    ("piece", 6, 7),
+    ("products", ((4, 2, True),)),
+    ("twin", 1, 0),
+    ("twin", 1, 1),
+    ("products", ((4, 1, False),)),
+    ("piece", 6, 6),
+    ("products", ((8, 1, True), (6, 0, True), (6, 1, False), (6, 2, True))),
 ]
 D = 768
 MEM = 256
@@ -160,7 +219,9 @@
 
     near = sorted({((sign * dx) % 4, (sign * dz) % 8) for dx, dz in STEPS for sign in (1, -1)})
     greet = [at(dx, dz) for dx, dz in near] + [at(0, 0, 0, True), at(0, 0, 1)]
-    greet += [device(x, y_hi, z, core, 1 - y_lo), device(x, 1 - y_hi, z, core, y_lo)]
+    greet += [device(x, y_hi, z, side, 1 - y_lo) for side in (core, 1 - core)]
+    greet += [device(x, 1 - y_hi, z, side, y_lo) for side in (core, 1 - core)]
+    greet.append(device(x, 1 - y_hi, z, 1 - core, 1 - y_lo))
     barrier = pltpu.get_barrier_semaphore()
     for one in greet:
         pl.semaphore_signal(barrier, inc=1, device_id=one, device_id_type=MESH)
@@ -231,10 +292,9 @@
     def landed(ref, sem):
         pltpu.make_async_remote_copy(ref, ref, send_sem.at[0], sem, device_id=at(0, 0, 1), device_id_type=MESH).wait_recv()
 
-    def forward(slot, q):
-        for s in range(1, N_SLOTS):
-            if ROUTE[s - 1][q] == slot:
-                push(held.at[piece(slot, q)], held.at[piece(s, q)], recv_sem.at[s * PIECES + q], at(AT[slot][0] - AT[s][0], AT[slot][1] - AT[s][1]))
+    def send(s, q):
+        slot = ROUTE[s - 1][q]
+        push(held.at[piece(slot, q)], held.at[piece(s, q)], recv_sem.at[s * PIECES + q], at(AT[slot][0] - AT[s][0], AT[slot][1] - AT[s][1]))
 
     def twin(slot, half):
         if slot in RIGHT:
@@ -243,7 +303,9 @@
 
     for q in range(HALF):
         push(give.at[q], held.at[y_hi * HALF + q], recv_sem.at[HALF + q], at(0, 0, 0, True))
-        forward(0, q)
+    first = [step[0] for step in PROGRAM].index("piece")
+    for step in PROGRAM[:first]:
+        send(*step[1:])
     twin(0, 0)
 
     loads[1].wait()
@@ -293,19 +355,18 @@
         else:
             lax.fori_loop(0, len(group), one, 0, unroll=True)
 
-    for step in PROGRAM:
-        if step[0] == "piece":
+    for step in PROGRAM[first:]:
+        if step[0] == "send":
+            send(*step[1:])
+        elif step[0] == "piece":
             s, q = step[1:]
             landed(held.at[piece(s, q)], recv_sem.at[s * PIECES + q])
-            forward(s, q)
             half = {("piece", s, r) for r in range(PIECES) if r // HALF == q // HALF}
             if half <= set(PROGRAM[: PROGRAM.index(step) + 1]):
                 twin(s, q // HALF)
         elif step[0] == "known":
-            for s in range(N_SLOTS):
-                for other in (0, 1):
-                    if s > 0 or other > 0:
-                        pl.semaphore_signal(known, inc=1, device_id=at(AT[s][0], AT[s][1], other), device_id_type=MESH)
+            for s in range(1, N_SLOTS):
+                pl.semaphore_signal(known, inc=1, device_id=at(AT[s][0], AT[s][1]), device_id_type=MESH)
         elif step[0] == "twin":
             s, half = step[1:]
             landed(held.at[pl.ds(BASE[s] * PIECES + PIECES + side_of(half) * HALF, HALF)], twin_sem.at[s * 2 + half])
@@ -324,7 +385,7 @@
     tell[:, 0, :] = turned[:BLOCKS]
     tell[:, 1, :] = turned[BLOCKS:]
 
-    pl.semaphore_wait(known, 2 * N_SLOTS - 1)
+    pl.semaphore_wait(known, N_SLOTS - 1)
 
     sender = (x * 8 + z) * 2 + core
     home = (y_hi * 8 + z) * 4 + core * 2 + y_lo

time: 44.5 us -> 43.8 us (0.984)
  Pallas kernels: 43.9 us -> 43.2 us
    pallas_call x1, Pallas kernels: 43.9 us -> 43.2 us  [on_device(): pl.pallas_call(kernel, out_shape=jax.ShapeDtypeStruct((1, MEM), F32), in_...]
where the time goes in v4:
time: 43.8 us; the launch traced here: 43.7 us
  Pallas kernels  43.2 us (99%)
  local copies, waits for them, and re-layouts  0.56 us (1%)
    pallas_call x1, Pallas kernels, on_device(): pl.pallas_call(kernel, out_shape=jax.ShapeDtypeStruct((1, MEM), F32), in_...  43.2 us

profile of v4, /device:TPU:1, one launch (start us, length us, event | category | flops | bytes accessed | tf_op | source)
XLA Modules:
  0.0 43.7 jit_solution(11955741805117046293)
XLA Ops:
  0.0 43.2 %shard_map.46 = f32[1,256]{1,0:T(1,128)S(1)} custom-call(bf16[2048,768]{1,0:T(8,128)(2,1)} %emb_hbm.1, s32[4,16384]{1,0:T(4,128)} %members_hbm.1, s32[4,16384]{1,0:T(4,128)} %order_hbm.1, s32[4]{0:T(128)} %sizes_hbm.1), custom_call_target="tpu_custom_call" | custom-call | flops 8589934592 | bytes 8388608 | tf_op jit(solution)/shard_map/pallas_call | solution.py:484
  43.2 0.6 %copy.6 = f32[256]{0:T(256)} copy(f32[256]{0:T(256)S(1)} %bitcast.1) | data formatting | bytes 2048

commit v5 on v4

--- a/solution.py
+++ b/solution.py
@@ -149,6 +149,7 @@
     ("piece", 4, 2),
     ("piece", 6, 2),
     ("products", ((8, 2, True), (8, 5, True))),
+    ("half", ((6, 0, True), (6, 2, True)), 0),
     ("piece", 4, 6),
     ("piece", 4, 5),
     ("piece", 6, 5),
@@ -160,7 +161,8 @@
     ("twin", 1, 1),
     ("products", ((4, 1, False),)),
     ("piece", 6, 6),
-    ("products", ((8, 1, True), (6, 0, True), (6, 1, False), (6, 2, True))),
+    ("products", ((8, 1, True), (6, 1, False))),
+    ("half", ((6, 0, True), (6, 2, True)), 1),
 ]
 D = 768
 MEM = 256
@@ -327,6 +329,32 @@
                 col_ord[r, :, 256 + hi * 128 : 256 + (hi + 1) * 128] = jnp.broadcast_to(line, (8, 128))
     col_best[...] = jnp.full(col_best.shape, -1.0, F32)
     row_best[...] = jnp.full(row_best.shape, -1.0, F32)
+
+    def half_products(group, half):
+        rows = pl.ds(pl.multiple_of(side_of(half) * 128, 128), 128)
+
+        def one(n, carry):
+            left = lookup(n, [LEFT.index(a) for a, b, full in group])
+            left_at = lookup(n, [BASE[a] * PIECES for a, b, full in group])
+            right = lookup(n, [RIGHT.index(b) for a, b, full in group])
+            right_at = lookup(n, [BASE[b] * PIECES for a, b, full in group])
+            column = lookup(n, [RIGHT.index(b) if full else len(RIGHT) for a, b, full in group])
+            a = held[pl.ds(left_at + side_of(half) * HALF, HALF)].reshape(128, D)
+            b = held[pl.ds(right_at, 2 * PIECES)].reshape(2 * MEM, D)
+            score = lax.dot_general(a, b, (((1,), (1,)), ((), ())), preferred_element_type=F32)
+            own = row_ord[left, rows, :]
+            best = row_best[left, rows, :]
+            for part in range(4):
+                lanes = slice(part * 128, (part + 1) * 128)
+                mine = score[:, lanes]
+                earlier = col_ord[right, 0:1, lanes] < own
+                best = jnp.maximum(best, jnp.where(earlier, mine, -1.0))
+                later = jnp.max(jnp.where(earlier, -1.0, mine).reshape(16, 8, 128), axis=0)
+                col_best[column, :, lanes] = jnp.maximum(col_best[column, :, lanes], later)
+            row_best[left, rows, :] = best
+            return carry
+
+        lax.fori_loop(0, len(group), one, 0, unroll=True)
 
     def products(group):
         def one(n, carry):
@@ -370,6 +398,8 @@
         elif step[0] == "twin":
             s, half = step[1:]
             landed(held.at[pl.ds(BASE[s] * PIECES + PIECES + side_of(half) * HALF, HALF)], twin_sem.at[s * 2 + half])
+        elif step[0] == "half":
+            half_products(*step[1:])
         else:
             products(step[1])
 

time: 43.8 us -> 43.9 us (level)
  no operation moved by 1% of the time
where the time goes in v5:
time: 43.9 us
  Pallas kernels  43.3 us (99%)
  local copies, waits for them, and re-layouts  0.56 us (1%)
    pallas_call x1, Pallas kernels, on_device(): pl.pallas_call(kernel, out_shape=jax.ShapeDtypeStruct((1, MEM), F32), in_...  43.3 us

profile of v5, /device:TPU:1, one launch (start us, length us, event | category | flops | bytes accessed | tf_op | source)
XLA Modules:
  0.0 43.9 jit_solution(2300800175965053049)
XLA Ops:
  0.0 43.3 %shard_map.46 = f32[1,256]{1,0:T(1,128)S(1)} custom-call(bf16[2048,768]{1,0:T(8,128)(2,1)} %emb_hbm.1, s32[4,16384]{1,0:T(4,128)} %members_hbm.1, s32[4,16384]{1,0:T(4,128)} %order_hbm.1, s32[4]{0:T(128)} %sizes_hbm.1), custom_call_target="tpu_custom_call" | custom-call | flops 8589934592 | bytes 8388608 | tf_op jit(solution)/shard_map/pallas_call | solution.py:514
  43.3 0.6 %copy.6 = f32[256]{0:T(256)} copy(f32[256]{0:T(256)S(1)} %bitcast.1) | data formatting | bytes 2048

commit v6 on v4

--- a/solution.py
+++ b/solution.py
@@ -421,7 +421,7 @@
 
         return carry
 
-    lax.fori_loop(0, len(FAR_FIRST), route, 0)
+    lax.fori_loop(0, len(FAR_FIRST), route, 0, unroll=True)
 
     block = home
     own_ids = members[pl.ds(x, 1), pl.ds(pl.multiple_of(block * MEM, MEM), MEM)]

time: 43.8 us -> 43.8 us (level)
  no operation moved by 1% of the time
where the time goes in v6:
time: 43.8 us; the launch traced here: 43.7 us
  Pallas kernels  43.1 us (98%)
  local copies, waits for them, and re-layouts  0.56 us (1%)
    pallas_call x1, Pallas kernels, on_device(): pl.pallas_call(kernel, out_shape=jax.ShapeDtypeStruct((1, MEM), F32), in_...  43.1 us

profile of v6, /device:TPU:1, one launch (start us, length us, event | category | flops | bytes accessed | tf_op | source)
XLA Modules:
  0.0 43.7 jit_solution(14238681211943103603)
XLA Ops:
  0.0 43.1 %shard_map.46 = f32[1,256]{1,0:T(1,128)S(1)} custom-call(bf16[2048,768]{1,0:T(8,128)(2,1)} %emb_hbm.1, s32[4,16384]{1,0:T(4,128)} %members_hbm.1, s32[4,16384]{1,0:T(4,128)} %order_hbm.1, s32[4]{0:T(128)} %sizes_hbm.1), custom_call_target="tpu_custom_call" | custom-call | flops 8589934592 | bytes 8388608 | tf_op jit(solution)/shard_map/pallas_call | solution.py:484
  43.2 0.6 %copy.6 = f32[256]{0:T(256)} copy(f32[256]{0:T(256)S(1)} %bitcast.1) | data formatting | bytes 2048
